TPU v7x, 512 devices: a whole 4x4x16 slice. The times are simulated.
512 devices in a mesh: dp: 32 (over z, core), fsdp: 16 (over x, y).
Axes of the slice: x: 4, y: 4, z: 16, core: 2. Of those that a mesh axis runs over, the one named last changes fastest.
Arguments:
- token_ids: int32 [65536], P(('dp', 'fsdp')), may hold values from 0 to 50431, as said below
- activations: bfloat16 [65536, 3072], P(('dp', 'fsdp'))
- grad_out: bfloat16 [65536, 3072], P(('dp', 'fsdp')), may hold values from -0.13183594 to 0.13183594
- error_buffer: bfloat16 [32, 3072, 3072], P('dp', 'fsdp'), may hold values from -6 to 6
- init_q: float32 [3072, 8], replicated, may hold values from -6 to 6
Outputs:
- p_factor: float32 [3072, 8], P('fsdp')
- q_factor: float32 [3072, 8], replicated
- error_next: bfloat16 [32, 3072, 3072], P('dp', 'fsdp')
Inputs may be any that keep to these rules, and one draw needn't show every extreme that they name: `token_ids`: id 1 is padding; on the rows of each device it forms a tail (possibly empty), and each device's first row holds id 0.
All inputs are finite; a program needn't handle non-finite values.
Results may differ from a plain program's by a relative error of at most 0.0006.
Values may be sent and summed in bfloat16 or wider, within the bound.
No kernel may reach another device: no remote copies, remote signals or barrier semaphores. Data moves between devices by JAX's collectives and lax.ppermute only.
A program may use at most 64 MiB of HBM per device.

v0:
```python
import jax
import jax.numpy as jnp
from jax import lax
from jax.sharding import PartitionSpec as P


def orthonormal_columns(p_rows):
    highest = lax.Precision.HIGHEST
    finished = []
    for index_col in range(p_rows.shape[1]):
        column = p_rows[:, index_col]
        if finished:
            stacked = jnp.stack(finished, axis=1)
            inner_vals = lax.psum(jnp.dot(column, stacked, precision=highest), "fsdp")
            column = column - jnp.dot(stacked, inner_vals, precision=highest)
        norm_square = lax.psum(jnp.sum(column * column), "fsdp")
        finished.append(column / jnp.sqrt(norm_square))
    return jnp.stack(finished, axis=1)


def on_device(token_ids, activations, grad_out, error_buffer, init_q):
    highest = lax.Precision.HIGHEST
    replicas = lax.axis_size("dp")
    valid_rows = (token_ids != 1).astype(grad_out.dtype)
    masked_grad = grad_out * valid_rows[:, None]
    x_cols = lax.all_to_all(activations, "fsdp", split_axis=1, concat_axis=0, tiled=True)
    error_rows = error_buffer[0]
    grad_rows = lax.dot_general(
        x_cols,
        lax.all_gather(masked_grad, "fsdp", axis=0, tiled=True),
        (((0,), (0,)), ((), ())),
        preferred_element_type=jnp.float32,
    )
    merged = grad_rows + error_rows.astype(jnp.float32)
    p_local = jnp.dot(merged, init_q, precision=highest)
    p_mean = lax.psum(p_local, "dp") / replicas
    ortho_basis = orthonormal_columns(p_mean)
    q_local = jnp.einsum(
        "rd,rk->dk", merged, ortho_basis, precision=highest, preferred_element_type=jnp.float32
    )
    q_factor = lax.psum(q_local, ("dp", "fsdp")) / replicas
    error_next = (merged - jnp.dot(ortho_basis, q_factor.T, precision=highest)).astype(jnp.bfloat16)
    return (ortho_basis, q_factor, error_next[None])


def solution(mesh):
    return jax.shard_map(
        on_device,
        mesh=mesh,
        in_specs=(
            P(("dp", "fsdp")),
            P(("dp", "fsdp"), None),
            P(("dp", "fsdp"), None),
            P("dp", "fsdp", None),
            P(),
        ),
        out_specs=(P("fsdp", None), P(), P("dp", "fsdp", None)),
        check_vma=False,
    )
```

profile of v0, /device:TPU:1, one launch (start us, length us, event | category | flops | bytes accessed | tf_op | source)
XLA Modules:
  0.0 1197.7 jit_solution(5980001329945168853)
XLA Ops:
  7.2 0.7 compare_convert_fusion
  8.0 2.1 broadcast_multiply_fusion
  10.6 19.1 %all_to_all.19 = bf16[128,16,192]{0,2,1:T(8,128)(2,1)S(1)} all-to-all(bf16[128,16,192]{0,2,1:T(8,128)(2,1)S(1)} %bitcast.83), channel_id=1, replica_groups=mesh['dp'=32,'fsdp'=16] {'fsdp'}, dimensions={1} | all-to-all | bytes 1572864 | tf_op jit(solution)/shard_map/all_to_all | solution.py:26
  29.7 92.6 %all-gather.2.cloned.1.call-done = bf16[2048,3072]{1,0:T(8,128)(2,1)} async-done(((bf16[128,3072]{1,0:T(8,128)(2,1)}), bf16[2048,3072]{1,0:T(8,128)(2,1)}) %all-gather.2.cloned.1.call-update) | async-done | bytes 12582928 | tf_op jit(solution)/shard_map/all_gather | solution.py:30
  122.3 7.6 fusion
  130.0 1.9 fusion.29
  131.9 48.0 %psum.119 = f32[192,8]{0,1:T(8,128)S(1)} all-reduce(f32[192,8]{0,1:T(8,128)S(1)} %fusion.29), channel_id=1, replica_groups=mesh['dp'=32,'fsdp'=16] {'dp'}, use_global_device_ids=true, to_apply=%region_0.0 | all-reduce | flops 1536 | bytes 12288 | tf_op jit(solution)/shard_map/psum | solution.py:36
  180.5 31.8 %psum.120 = f32[]{:T(128)} all-reduce(f32[]{:T(128)} %multiply_reduce_fusion.8), channel_id=1, replica_groups=mesh['dp'=32,'fsdp'=16] {'fsdp'}, use_global_device_ids=true, to_apply=%region_2.0 | all-reduce | flops 1 | bytes 8 | tf_op jit(solution)/shard_map/psum | solution.py:16
  213.6 29.1 %psum.121 = f32[]{:T(128)} all-reduce(f32[]{:T(128)} %multiply_reduce_fusion), channel_id=1, replica_groups=mesh['dp'=32,'fsdp'=16] {'fsdp'}, use_global_device_ids=true, to_apply=%region_3.0 | all-reduce | flops 1 | bytes 8 | tf_op jit(solution)/shard_map/psum | solution.py:14
  242.8 1.2 multiply_reduce_fusion.7
  244.0 30.6 %psum.122 = f32[]{:T(128)} all-reduce(f32[]{:T(128)} %multiply_reduce_fusion.7), channel_id=1, replica_groups=mesh['dp'=32,'fsdp'=16] {'fsdp'}, use_global_device_ids=true, to_apply=%region_5.0 | all-reduce | flops 1 | bytes 8 | tf_op jit(solution)/shard_map/psum | solution.py:16
  275.3 0.7 broadcast_divide_fusion.6
  276.1 29.1 %psum.123 = f32[2]{0:T(128)S(1)} all-reduce(f32[2]{0:T(128)S(1)} %convolution_bitcast_fusion.6), channel_id=1, replica_groups=mesh['dp'=32,'fsdp'=16] {'fsdp'}, use_global_device_ids=true, to_apply=%region_6.0 | all-reduce | flops 2 | bytes 16 | tf_op jit(solution)/shard_map/psum | solution.py:14
  305.3 0.6 multiply_reduce_fusion.6
  305.9 30.0 %psum.124 = f32[]{:T(128)} all-reduce(f32[]{:T(128)} %get-tuple-element.13), channel_id=1, replica_groups=mesh['dp'=32,'fsdp'=16] {'fsdp'}, use_global_device_ids=true, to_apply=%region_8.0 | all-reduce | flops 1 | bytes 8 | tf_op jit(solution)/shard_map/psum | solution.py:16
  336.7 29.1 %psum.125 = f32[3]{0:T(128)S(1)} all-reduce(f32[3]{0:T(128)S(1)} %convolution_bitcast_fusion.5), channel_id=1, replica_groups=mesh['dp'=32,'fsdp'=16] {'fsdp'}, use_global_device_ids=true, to_apply=%region_9.0 | all-reduce | flops 3 | bytes 24 | tf_op jit(solution)/shard_map/psum | solution.py:14
  366.5 30.0 %psum.126 = f32[]{:T(128)} all-reduce(f32[]{:T(128)} %get-tuple-element.11), channel_id=1, replica_groups=mesh['dp'=32,'fsdp'=16] {'fsdp'}, use_global_device_ids=true, to_apply=%region_11.0 | all-reduce | flops 1 | bytes 8 | tf_op jit(solution)/shard_map/psum | solution.py:16
  397.3 29.5 %psum.127 = f32[4]{0:T(128)S(1)} all-reduce(f32[4]{0:T(128)S(1)} %convolution_bitcast_fusion.4), channel_id=1, replica_groups=mesh['dp'=32,'fsdp'=16] {'fsdp'}, use_global_device_ids=true, to_apply=%region_12.0 | all-reduce | flops 4 | bytes 32 | tf_op jit(solution)/shard_map/psum | solution.py:14
  427.6 29.6 %psum.128 = f32[]{:T(128)} all-reduce(f32[]{:T(128)} %get-tuple-element.9), channel_id=1, replica_groups=mesh['dp'=32,'fsdp'=16] {'fsdp'}, use_global_device_ids=true, to_apply=%region_14.0 | all-reduce | flops 1 | bytes 8 | tf_op jit(solution)/shard_map/psum | solution.py:16
  458.0 29.8 %psum.129 = f32[5]{0:T(128)S(1)} all-reduce(f32[5]{0:T(128)S(1)} %convolution_bitcast_fusion.3), channel_id=1, replica_groups=mesh['dp'=32,'fsdp'=16] {'fsdp'}, use_global_device_ids=true, to_apply=%region_15.0 | all-reduce | flops 5 | bytes 40 | tf_op jit(solution)/shard_map/psum | solution.py:14
  487.9 0.6 multiply_reduce_fusion.3
  488.5 29.3 %psum.130 = f32[]{:T(128)} all-reduce(f32[]{:T(128)} %get-tuple-element.7), channel_id=1, replica_groups=mesh['dp'=32,'fsdp'=16] {'fsdp'}, use_global_device_ids=true, to_apply=%region_17.0 | all-reduce | flops 1 | bytes 8 | tf_op jit(solution)/shard_map/psum | solution.py:16
  518.7 30.6 %psum.131 = f32[6]{0:T(128)S(1)} all-reduce(f32[6]{0:T(128)S(1)} %convolution_bitcast_fusion.2), channel_id=1, replica_groups=mesh['dp'=32,'fsdp'=16] {'fsdp'}, use_global_device_ids=true, to_apply=%region_18.0 | all-reduce | flops 6 | bytes 48 | tf_op jit(solution)/shard_map/psum | solution.py:14
  549.4 0.6 multiply_reduce_fusion.2
  550.0 29.3 %psum.132 = f32[]{:T(128)} all-reduce(f32[]{:T(128)} %get-tuple-element.5), channel_id=1, replica_groups=mesh['dp'=32,'fsdp'=16] {'fsdp'}, use_global_device_ids=true, to_apply=%region_20.0 | all-reduce | flops 1 | bytes 8 | tf_op jit(solution)/shard_map/psum | solution.py:16
  580.2 30.5 %psum.133 = f32[7]{0:T(128)S(1)} all-reduce(f32[7]{0:T(128)S(1)} %convolution_bitcast_fusion.1), channel_id=1, replica_groups=mesh['dp'=32,'fsdp'=16] {'fsdp'}, use_global_device_ids=true, to_apply=%region_21.0 | all-reduce | flops 7 | bytes 56 | tf_op jit(solution)/shard_map/psum | solution.py:14
  610.9 0.6 multiply_reduce_fusion.1
  611.5 29.1 %psum.134 = f32[]{:T(128)} all-reduce(f32[]{:T(128)} %get-tuple-element.3), channel_id=1, replica_groups=mesh['dp'=32,'fsdp'=16] {'fsdp'}, use_global_device_ids=true, to_apply=%region_23.0 | all-reduce | flops 1 | bytes 8 | tf_op jit(solution)/shard_map/psum | solution.py:16
  641.3 2.0 fusion.30
  643.3 543.5 %all-reduce.2.cloned.1.call-done = f32[3072,8]{0,1:T(8,128)} async-done(((f32[3072,8]{0,1:T(8,128)}), f32[3072,8]{0,1:T(8,128)}) %all-reduce.2.cloned.1.call-update) | async-done | bytes 98320 | tf_op jit(solution)/shard_map/psum | solution.py:41
  1186.9 0.9 broadcast_multiply_fusion.1
  1187.8 3.1 fusion.2
  (41 shorter events, 4.7 us)
Async XLA Ops:
  7.2 122.8 %copy-start = (f32[3072,8]{0,1:T(8,128)S(1)}, f32[3072,8]{0,1:T(8,128)}, u32[]{:S(2)}) copy-start(f32[3072,8]{0,1:T(8,128)} %param.9) | copy-start | bytes 294916
  7.2 3.0 copy-start.1
  7.2 115.1 %all-gather.2.cloned.1.call-start = ((), (), s32[]{:S(2)}) async-start(), calls=%async_computation.1 | async-start | bytes 13369344 | tf_op jit(solution)/shard_map/all_gather | solution.py:30
  10.1 1176.7 %all-reduce.2.cloned.1.call-start = ((), (), s32[]{:S(2)}) async-start(), calls=%async_computation.2 | async-start | bytes 196608 | tf_op jit(solution)/shard_map/psum | solution.py:41
  641.3 549.5 %copy-start.3 = (f32[192,8]{0,1:T(8,128)}, f32[192,8]{0,1:T(8,128)S(1)}, u32[]{:S(2)}) copy-start(f32[192,8]{0,1:T(8,128)S(1)} %stack.41) | copy-start | bytes 18436
  1187.8 3.1 copy-start.2
Sparse Core Ops, SparseCore 0:
  11.7 110.6 all-gather.1
  643.4 543.3 all-reduce.1
where the time goes:
time: 1200 us
  waiting for transfers between devices  636 us (53%)
  blocking collectives  514 us (43%)
  between operations  19.7 us (2%)
  matrix products  16.2 us (1%)
    psum x1, waiting for transfers between devices, on_device(): q_factor = lax.psum(q_local, ('dp', 'fsdp')) / replicas  544 us
    psum x8, blocking collectives, orthonormal_columns(): norm_square = lax.psum(jnp.sum(column * column), 'fsdp')  240 us
    psum x7, blocking collectives, orthonormal_columns(): inner_vals = lax.psum(jnp.dot(column, stacked, precision=highest), 'fsdp')  208 us
    all_gather x1, waiting for transfers between devices, on_device(): lax.all_gather(masked_grad, 'fsdp', axis=0, tiled=True)  92.6 us
    psum x1, blocking collectives, on_device(): p_mean = lax.psum(p_local, 'dp') / replicas  48 us
  transfers between devices with their start and end apart: 2, of which 2 were waited for; matrix products, arithmetic and copies ran while one was open for 0% of the time, Pallas kernels for 0%

commit v1 on v0

--- a/solution.py
+++ b/solution.py
@@ -1,7 +1,15 @@
+import functools
 import jax
 import jax.numpy as jnp
 from jax import lax
 from jax.sharding import PartitionSpec as P
+
+
+def put_frame(load, mesh_name):
+    return jax.lax.all_gather(load, mesh_name).sum(axis=0)
+
+
+_finish_circles = functools.partial(put_frame, mesh_name="fsdp")
 
 
 def orthonormal_columns(p_rows):
@@ -11,7 +19,7 @@
         column = p_rows[:, index_col]
         if finished:
             stacked = jnp.stack(finished, axis=1)
-            inner_vals = lax.psum(jnp.dot(column, stacked, precision=highest), "fsdp")
+            inner_vals = _finish_circles(jnp.dot(column, stacked, precision=highest))
             column = column - jnp.dot(stacked, inner_vals, precision=highest)
         norm_square = lax.psum(jnp.sum(column * column), "fsdp")
         finished.append(column / jnp.sqrt(norm_square))

time: 1200 us -> 1200 us (level)
  blocking collectives: 514 us -> 495 us
    psum x7 -> x0, blocking collectives: 208 us -> none  [orthonormal_columns(): inner_vals = lax.psum(jnp.dot(column, stacked, precision=highest), 'fsdp')]
    unnamed x0 -> x7, blocking collectives: none -> 207 us
    all_to_all x1 -> x0, blocking collectives: 19.1 us -> none  [on_device(): lax.all_to_all(activations, 'fsdp', split_axis=1, concat_axis=0, tiled=True)]
  transfers between devices with their start and end apart: 2 -> 3, of which waited for: 2 -> 3; matrix products, arithmetic and copies ran while one was open for 0% -> 0% of each run, Pallas kernels for 0% -> 0%
where the time goes in v1:
time: 1200 us
  waiting for transfers between devices  644 us (54%)
  blocking collectives  495 us (41%)
  between operations  23.7 us (2%)
  matrix products  16 us (1%)
    psum x1, waiting for transfers between devices, on_device(): q_factor = lax.psum(q_local, ('dp', 'fsdp')) / replicas  543 us
    psum x8, blocking collectives, orthonormal_columns(): norm_square = lax.psum(jnp.sum(column * column), 'fsdp')  240 us
    unnamed x7, blocking collectives  207 us
    all_gather x1, waiting for transfers between devices, on_device(): lax.all_gather(masked_grad, 'fsdp', axis=0, tiled=True)  92.7 us
    psum x1, blocking collectives, on_device(): p_mean = lax.psum(p_local, 'dp') / replicas  48 us
  transfers between devices with their start and end apart: 3, of which 3 were waited for; matrix products, arithmetic and copies ran while one was open for 0% of the time, Pallas kernels for 0%

profile of v1, /device:TPU:1, one launch (start us, length us, event | category | flops | bytes accessed | tf_op | source)
XLA Modules:
  0.0 1202.9 jit_solution(4406290757717115242)
XLA Ops:
  7.2 0.7 compare_convert_fusion
  8.0 2.1 broadcast_multiply_fusion
  10.1 1.2 copy.8
  11.3 7.6 all-to-all-start
  19.0 1.3 dynamic-slice
  22.2 7.4 all-to-all-done
  29.6 92.7 %all-gather.8.cloned.1.call-done = bf16[2048,3072]{1,0:T(8,128)(2,1)} async-done(((bf16[128,3072]{1,0:T(8,128)(2,1)}), bf16[2048,3072]{1,0:T(8,128)(2,1)}) %all-gather.8.cloned.1.call-update) | async-done | bytes 12582928 | tf_op jit(solution)/shard_map/all_gather | solution.py:38
  122.3 7.5 fusion
  129.8 1.9 fusion.29
  131.7 48.0 %psum.70 = f32[192,8]{0,1:T(8,128)S(1)} all-reduce(f32[192,8]{0,1:T(8,128)S(1)} %fusion.29), channel_id=1, replica_groups=mesh['dp'=32,'fsdp'=16] {'dp'}, use_global_device_ids=true, to_apply=%region_0.0 | all-reduce | flops 1536 | bytes 12288 | tf_op jit(solution)/shard_map/psum | solution.py:44
  181.0 31.8 %psum.71 = f32[]{:T(128)} all-reduce(f32[]{:T(128)} %multiply_reduce_fusion.8), channel_id=1, replica_groups=mesh['dp'=32,'fsdp'=16] {'fsdp'}, use_global_device_ids=true, to_apply=%region_2.0 | all-reduce | flops 1 | bytes 8 | tf_op jit(solution)/shard_map/psum | solution.py:24
  214.2 1.4 dynamic-update-slice
  216.2 28.5 %all-reduce = f32[16]{0:T(128)S(1)} all-reduce(f32[16]{0:T(128)S(1)} %dynamic-update-slice), channel_id=1, replica_groups=mesh['dp'=32,'fsdp'=16] {'fsdp'}, use_global_device_ids=true, to_apply=%add | all-reduce | flops 16 | bytes 128
  245.3 1.2 multiply_reduce_fusion.7
  247.2 30.6 %psum.72 = f32[]{:T(128)} all-reduce(f32[]{:T(128)} %multiply_reduce_fusion.7), channel_id=1, replica_groups=mesh['dp'=32,'fsdp'=16] {'fsdp'}, use_global_device_ids=true, to_apply=%region_5.0 | all-reduce | flops 1 | bytes 8 | tf_op jit(solution)/shard_map/psum | solution.py:24
  278.5 0.7 broadcast_divide_fusion.6
  279.5 29.4 %all-reduce.1 = f32[32]{0:T(128)S(1)} all-reduce(f32[32]{0:T(128)S(1)} %dynamic-update-slice.1), channel_id=2, replica_groups=mesh['dp'=32,'fsdp'=16] {'fsdp'}, use_global_device_ids=true, to_apply=%add.1 | all-reduce | flops 32 | bytes 256
  309.8 29.9 %psum.73 = f32[]{:T(128)} all-reduce(f32[]{:T(128)} %get-tuple-element.13), channel_id=1, replica_groups=mesh['dp'=32,'fsdp'=16] {'fsdp'}, use_global_device_ids=true, to_apply=%region_8.0 | all-reduce | flops 1 | bytes 8 | tf_op jit(solution)/shard_map/psum | solution.py:24
  340.8 29.3 %all-reduce.2 = f32[48]{0:T(128)S(1)} all-reduce(f32[48]{0:T(128)S(1)} %dynamic-update-slice.2), channel_id=3, replica_groups=mesh['dp'=32,'fsdp'=16] {'fsdp'}, use_global_device_ids=true, to_apply=%add.2 | all-reduce | flops 48 | bytes 384
  371.0 30.0 %psum.74 = f32[]{:T(128)} all-reduce(f32[]{:T(128)} %get-tuple-element.11), channel_id=1, replica_groups=mesh['dp'=32,'fsdp'=16] {'fsdp'}, use_global_device_ids=true, to_apply=%region_11.0 | all-reduce | flops 1 | bytes 8 | tf_op jit(solution)/shard_map/psum | solution.py:24
  402.0 29.6 %all-reduce.3 = f32[64]{0:T(128)S(1)} all-reduce(f32[64]{0:T(128)S(1)} %dynamic-update-slice.3), channel_id=4, replica_groups=mesh['dp'=32,'fsdp'=16] {'fsdp'}, use_global_device_ids=true, to_apply=%add.3 | all-reduce | flops 64 | bytes 512
  432.5 29.4 %psum.75 = f32[]{:T(128)} all-reduce(f32[]{:T(128)} %get-tuple-element.9), channel_id=1, replica_groups=mesh['dp'=32,'fsdp'=16] {'fsdp'}, use_global_device_ids=true, to_apply=%region_14.0 | all-reduce | flops 1 | bytes 8 | tf_op jit(solution)/shard_map/psum | solution.py:24
  463.0 29.8 %all-reduce.4 = f32[80]{0:T(128)S(1)} all-reduce(f32[80]{0:T(128)S(1)} %dynamic-update-slice.4), channel_id=5, replica_groups=mesh['dp'=32,'fsdp'=16] {'fsdp'}, use_global_device_ids=true, to_apply=%add.4 | all-reduce | flops 80 | bytes 640
  493.7 29.2 %psum.76 = f32[]{:T(128)} all-reduce(f32[]{:T(128)} %get-tuple-element.7), channel_id=1, replica_groups=mesh['dp'=32,'fsdp'=16] {'fsdp'}, use_global_device_ids=true, to_apply=%region_17.0 | all-reduce | flops 1 | bytes 8 | tf_op jit(solution)/shard_map/psum | solution.py:24
  524.0 30.5 %all-reduce.5 = f32[96]{0:T(128)S(1)} all-reduce(f32[96]{0:T(128)S(1)} %dynamic-update-slice.5), channel_id=6, replica_groups=mesh['dp'=32,'fsdp'=16] {'fsdp'}, use_global_device_ids=true, to_apply=%add.5 | all-reduce | flops 96 | bytes 768
  555.4 29.4 %psum.77 = f32[]{:T(128)} all-reduce(f32[]{:T(128)} %get-tuple-element.5), channel_id=1, replica_groups=mesh['dp'=32,'fsdp'=16] {'fsdp'}, use_global_device_ids=true, to_apply=%region_20.0 | all-reduce | flops 1 | bytes 8 | tf_op jit(solution)/shard_map/psum | solution.py:24
  585.9 29.8 %all-reduce.6 = f32[112]{0:T(128)S(1)} all-reduce(f32[112]{0:T(128)S(1)} %dynamic-update-slice.6), channel_id=7, replica_groups=mesh['dp'=32,'fsdp'=16] {'fsdp'}, use_global_device_ids=true, to_apply=%add.6 | all-reduce | flops 112 | bytes 896
  616.6 29.2 %psum.78 = f32[]{:T(128)} all-reduce(f32[]{:T(128)} %get-tuple-element.3), channel_id=1, replica_groups=mesh['dp'=32,'fsdp'=16] {'fsdp'}, use_global_device_ids=true, to_apply=%region_23.0 | all-reduce | flops 1 | bytes 8 | tf_op jit(solution)/shard_map/psum | solution.py:24
  646.6 2.0 fusion.30
  648.6 543.5 %all-reduce.9.cloned.1.call-done = f32[3072,8]{0,1:T(8,128)} async-done(((f32[3072,8]{0,1:T(8,128)}), f32[3072,8]{0,1:T(8,128)}) %all-reduce.9.cloned.1.call-update) | async-done | bytes 98320 | tf_op jit(solution)/shard_map/psum | solution.py:49
  1192.0 0.9 broadcast_multiply_fusion.1
  1192.9 3.1 fusion.2
  (70 shorter events, 9.3 us)
Async XLA Ops:
  7.2 122.6 %copy-start = (f32[3072,8]{0,1:T(8,128)S(1)}, f32[3072,8]{0,1:T(8,128)}, u32[]{:S(2)}) copy-start(f32[3072,8]{0,1:T(8,128)} %param.9) | copy-start | bytes 294916
  7.2 2.9 copy-start.1
  7.2 115.1 %all-gather.8.cloned.1.call-start = ((), (), s32[]{:S(2)}) async-start(), calls=%async_computation.1 | async-start | bytes 13369344 | tf_op jit(solution)/shard_map/all_gather | solution.py:38
  11.3 18.3 %all-to-all-start = ((bf16[128,16,192]{0,2,1:T(8,128)(2,1)}), bf16[128,16,192]{0,2,1:T(8,128)(2,1)S(1)}, u32[]{:S(2)}, u32[]{:S(2)}) async-start(bf16[128,16,192]{0,2,1:T(8,128)(2,1)} %bitcast), calls=%async_computation | async-start | bytes 1572864 | tf_op jit(solution)/shard_map/all_to_all | solution.py:34
  18.9 1173.1 %all-reduce.9.cloned.1.call-start = ((), (), s32[]{:S(2)}) async-start(), calls=%async_computation.2 | async-start | bytes 196608 | tf_op jit(solution)/shard_map/psum | solution.py:49
  646.6 549.5 %copy-start.3 = (f32[192,8]{0,1:T(8,128)}, f32[192,8]{0,1:T(8,128)S(1)}, u32[]{:S(2)}) copy-start(f32[192,8]{0,1:T(8,128)S(1)} %stack.41) | copy-start | bytes 18436
  1192.9 3.1 copy-start.2
Sparse Core Ops, SparseCore 0:
  11.7 110.6 all-gather.7
  648.7 543.3 all-reduce.8
